TPU v7x, 32 devices: a whole 2x2x4 slice. The times are simulated.
32 devices in a mesh: seq: 8 (over z, x), tensor: 4 (over y, core).
Axes of the slice: x: 2, y: 2, z: 4, core: 2. Of those that a mesh axis runs over, the one named last changes fastest.
Arguments:
- features: bfloat16 [16, 7168], P(None, 'seq'), may hold values from -300 to 300
- input_norm_scale: float32 [7168], P('seq'), may hold values from 0.25 to 1.75
- query_key_value_weight: bfloat16 [7168, 3, 7168], P('seq', None, 'tensor'), may hold values from -0.0625 to 0.0625
- adapter_down_weight: bfloat16 [7168, 128], P('seq'), may hold values from -0.0625 to 0.0625
- adapter_up_weight: bfloat16 [128, 7168], P(None, 'tensor'), may hold values from -0.5 to 0.5
- output_weight: bfloat16 [7168, 3584], P('tensor', 'seq'), may hold values from -0.0625 to 0.0625
- cached_key_rows: bfloat16 [4, 4096, 7168], P(None, 'seq', 'tensor'), may hold values from -400 to 400
- cached_value_rows: bfloat16 [4, 4096, 7168], P(None, 'seq', 'tensor'), may hold values from -6 to 6
- lengths: int32 [4], replicated, may hold values from 16 to 4092, as said below
- sinks: int32 [4], replicated, may hold values from 1 to 4, as said below
- windows: int32 [4], replicated, may hold values from 512 to 1024, as said below
Outputs:
- mixed: float32 [16, 3584], P(None, 'seq')
- new_kv: float32 [2, 16, 7168], P(None, None, 'tensor')
Inputs may be any that keep to these rules, and one draw needn't show every extreme that they name: `lengths`: heavy-tailed; at least one request has 4092. `sinks`: at least one request has 4. `windows`: at least one request has 1024.
All inputs are finite; a program needn't handle non-finite values.
Results may differ from a plain program's by a relative error of at most 0.022.
Values sent between devices are 32-bit elements; how exact they have to be, the bound alone decides.
A program may use at most 128 MiB of HBM per device.

v0:
```python
import jax
import jax.numpy as jnp
from jax import lax
from jax.sharding import PartitionSpec as P

HD = 224
NEW = 4
INPUT_WIDTH = 7168


NEG = -1e30
CUT = -1e29


def row_stats(partial_low_rank, partial_sq):
    return lax.psum((partial_low_rank, partial_sq), "seq")


def live_block(base, span, length, sink, window):
    return (base < length) & ((base < sink) | (base + span - 1 > length - window))


def cache_scores(query_all, cached_key_rows, lengths, sinks, windows, base):
    count, span = (cached_key_rows.shape[0], cached_key_rows.shape[1])
    heads = query_all.shape[2]
    position = base + jnp.arange(span, dtype=jnp.int32)
    order = jnp.arange(NEW, dtype=jnp.int32)

    def score_one(index):
        length = lengths[index]
        sink = sinks[index]
        window = windows[index]

        def score_compute():
            keys = cached_key_rows[index].reshape(span, heads, HD)
            raw = jnp.einsum(
                "thd,phd->htp", query_all[index], keys, preferred_element_type=jnp.float32
            ) * HD ** (-0.5)
            seen = (position[None, :] < length) & (
                (position[None, :] < sink) | (length + order[:, None] - position[None, :] < window)
            )
            return jnp.where(seen[None], raw, NEG)

        def score_skipped():
            return jnp.full((heads, NEW, span), NEG, jnp.float32)

        return lax.cond(live_block(base, span, length, sink, window), score_compute, score_skipped)

    return lax.map(score_one, jnp.arange(count, dtype=jnp.int32))


def cache_terms(scores, cached_value_rows, top, lengths, sinks, windows, base):
    count, span = (cached_value_rows.shape[0], cached_value_rows.shape[1])
    heads = scores.shape[1]

    def weigh_one(index):

        def weigh_compute():
            expo = jnp.where(
                scores[index] > CUT, jnp.exp(scores[index] - top[index][..., None]), 0.0
            )
            values = cached_value_rows[index].reshape(span, heads, HD)
            output = jnp.einsum(
                "htp,phd->htd",
                expo.astype(jnp.bfloat16),
                values,
                preferred_element_type=jnp.float32,
            )
            return (jnp.sum(expo, axis=-1), output)

        def weigh_skipped():
            return (jnp.zeros((heads, NEW), jnp.float32), jnp.zeros((heads, NEW, HD), jnp.float32))

        return lax.cond(
            live_block(base, span, lengths[index], sinks[index], windows[index]),
            weigh_compute,
            weigh_skipped,
        )

    return lax.map(weigh_one, jnp.arange(count, dtype=jnp.int32))


def own_scores(query_all, key_all):
    raw = jnp.einsum(
        "rthd,ruhd->rhtu", query_all, key_all, preferred_element_type=jnp.float32
    ) * HD ** (-0.5)
    order = jnp.arange(NEW, dtype=jnp.int32)
    causal = order[:, None] >= order[None, :]
    return jnp.where(causal[None, None], raw, NEG)


def own_terms(fresh, value_all, top):
    expo = jnp.where(fresh > CUT, jnp.exp(fresh - top[..., None]), 0.0)
    output = jnp.einsum(
        "rhtu,ruhd->rhtd", expo.astype(jnp.bfloat16), value_all, preferred_element_type=jnp.float32
    )
    return (jnp.sum(expo, axis=-1), output)


def shards(
    features,
    input_norm_scale,
    query_key_value_weight,
    adapter_down_weight,
    adapter_up_weight,
    output_weight,
    cached_key_rows,
    cached_value_rows,
    lengths,
    sinks,
    windows,
):
    rows = features.shape[0]
    count = cached_key_rows.shape[0]
    local_attention = adapter_up_weight.shape[1]
    heads = local_attention // HD
    feat = features.astype(jnp.float32)
    scaled_scores = (feat * input_norm_scale).astype(jnp.bfloat16)
    weights = query_key_value_weight.reshape(query_key_value_weight.shape[0], 3 * local_attention)
    partial_low_rank = jnp.dot(
        scaled_scores, adapter_down_weight, preferred_element_type=jnp.float32
    )
    partial_sq = jnp.sum(feat * feat, axis=1)
    partial_proj = jnp.dot(scaled_scores, weights, preferred_element_type=jnp.float32)
    low_rank_query, total_sq = row_stats(partial_low_rank, partial_sq)
    scale_rows = lax.rsqrt(total_sq / INPUT_WIDTH + 1e-05)[:, None]
    lowrank = (low_rank_query * scale_rows).astype(jnp.bfloat16)
    query_adapter = jnp.dot(lowrank, adapter_up_weight, preferred_element_type=jnp.float32)
    projected = lax.psum(partial_proj, "seq")
    queries = (projected[:, :local_attention] * scale_rows + query_adapter).astype(jnp.bfloat16)
    keys_full = projected[:, local_attention : 2 * local_attention] * scale_rows
    values_full = projected[:, 2 * local_attention :] * scale_rows
    new_keys = keys_full.astype(jnp.bfloat16)
    new_values = values_full.astype(jnp.bfloat16)
    base = lax.axis_index("seq") * cached_key_rows.shape[1]
    query_all = queries.reshape(count, NEW, heads, HD)
    key_all = new_keys.reshape(count, NEW, heads, HD)
    value_all = new_values.reshape(count, NEW, heads, HD)
    scores = cache_scores(query_all, cached_key_rows, lengths, sinks, windows, base)
    fresh = own_scores(query_all, key_all)
    local_top = jnp.maximum(jnp.max(scores, axis=-1), jnp.max(fresh, axis=-1))
    top = lax.pmax(local_top, "seq")
    total, output = cache_terms(scores, cached_value_rows, top, lengths, sinks, windows, base)
    total, output = lax.psum((total, output), "seq")
    own_total, own_output = own_terms(fresh, value_all, top)
    total = total + own_total
    output = output + own_output
    attn = (
        (output / total[..., None])
        .transpose(0, 2, 1, 3)
        .reshape(rows, local_attention)
        .astype(jnp.bfloat16)
    )
    partial_out = jnp.dot(attn, output_weight, preferred_element_type=jnp.float32)
    mixed = lax.psum(partial_out, "tensor")
    return (mixed, jnp.stack([keys_full, values_full]))


def solution(mesh):
    in_specs = (
        P(None, "seq"),
        P("seq"),
        P("seq", None, "tensor"),
        P("seq", None),
        P(None, "tensor"),
        P("tensor", "seq"),
        P(None, "seq", "tensor"),
        P(None, "seq", "tensor"),
        P(),
        P(),
        P(),
    )
    out_specs = (P(None, "seq"), P(None, None, "tensor"))
    return jax.shard_map(shards, mesh=mesh, in_specs=in_specs, out_specs=out_specs, check_vma=False)
```

profile of v0, /device:TPU:0, one launch (start us, length us, event | category | flops | bytes accessed | tf_op | source)
XLA Modules:
  0.0 329.2 jit_solution(8999206060914383240)
XLA Ops:
  7.2 13.4 %copy.50 = bf16[896,3,1792]{0,2,1:T(8,128)(2,1)} copy(bf16[896,3,1792]{2,0,1:T(8,128)(2,1)} %param.21) | data formatting | bytes 19267584 | tf_op args[2]
  20.7 7.2 %fusion.33 = f32[16,5376]{1,0:T(8,128)} fusion(bf16[896,5376]{0,1:T(8,128)(2,1)} %bitcast.69, bf16[16,896]{1,0:T(8,128)(2,1)S(1)} %copy-done.2, f32[896]{0:T(1024)S(1)} %copy-done.4), kind=kOutput, calls=%fused_computation.55 | convolution fusion | flops 154183680 | bytes 10010112 | tf_op jit(solution)/shard_map/dot_general | solution.py:124
  28.2 23.7 %all-reduce = (f32[16]{0:T(128)S(1)}, f32[16,128]{1,0:T(8,128)S(1)}) all-reduce(f32[16]{0:T(128)S(1)} %fusion.29, f32[16,128]{1,0:T(8,128)S(1)} %fusion.31), channel_id=1, replica_groups=mesh['seq'=8,'tensor'=4] {'seq'}, use_global_device_ids=true, to_apply=%region_2.0 | all-reduce | flops 2064 | bytes 16512 | tf_op jit(solution)/shard_map/psum | solution.py:16
  51.9 10.0 %copy.52 = bf16[4,512,1792]{1,2,0:T(8,128)(2,1)} copy(bf16[4,512,1792]{2,1,0:T(8,128)(2,1)} %param.25) | data formatting | bytes 14680064
  61.9 10.0 %copy.58 = bf16[4,512,1792]{1,2,0:T(8,128)(2,1)} copy(bf16[4,512,1792]{2,1,0:T(8,128)(2,1)} %param.26) | data formatting | bytes 14680064 | tf_op jit(solution)/shard_map/while | solution.py:80
  71.9 30.2 %all-reduce.4.cloned.1.call-done = f32[16,5376]{1,0:T(8,128)} async-done(((f32[16,5376]{1,0:T(8,128)}), f32[16,5376]{1,0:T(8,128)}) %all-reduce.4.cloned.1.call-update) | async-done | bytes 344080 | tf_op jit(solution)/shard_map/psum | solution.py:129
  102.1 1.0 fusion.21
  103.3 1.1 fusion.17
  105.2 55.7 %while.31 = (s32[]{:T(128)}, f32[4,8,4,512]{3,2,1,0:T(4,128)S(1)}, s32[4]{0:T(128)S(1)}, s32[4]{0:T(128)S(1)}, s32[]{:T(128)}, /*index=5*/s32[4]{0:T(128)S(1)}, ...) while((s32[]{:T(128)}, f32[4,8,4,512]{3,2,1,0:T(4,128)S(1)}, ...), condition=%wide.region_7.8_spmd.clone.clone.clone, body=%wide.region_4.7_spmd.clone.clone.clone.sunk | while | flops 7382547 | bytes 5734851 | solution.py:49
  105.2 0.7 dynamic_slice.98
  107.8 0.7 dynamic_slice.99
  109.0 0.7 dynamic_slice.101
  112.4 6.7 %conditional.8 = (f32[1,8,4,512]{3,2,1,0:T(4,128)S(1)}) conditional(s32[]{:T(128)} %convert_element_type.82, () %tuple.106, (s32[]{:T(128)}, s32[]{:T(128)}, s32[]{:T(128)}, s32[4]{0:T(128)S(1)}, s32[]{:T(128)}, /*index=5*/s32[]{:T(128)}, bf16[4,4,8,224]{3,1,2,0:T(4,128)(2,1)S(1)}, bf16[4,512,1792]{1,2,0:T(8,128)(2,1)}, s32[512]{0:T(512)S(1)}) %tuple.107), branch_computations={%region_5.5_spmd, %region_6.6_spmd} | conditional | flops 7382535 | bytes 5601398 | solution.py:47
  112.4 0.7 broadcast_compare_fusion.1
  113.1 0.6 broadcast_compare_fusion
  113.8 0.7 broadcast_add_fusion.1
  114.5 0.8 fusion.7
  117.1 1.6 constant_dynamic-slice_fusion
  119.1 0.7 dynamic_slice.98
  121.7 0.7 dynamic_slice.99
  123.0 0.7 dynamic_slice.101
  126.3 6.7 %conditional.8 = (f32[1,8,4,512]{3,2,1,0:T(4,128)S(1)}) conditional(s32[]{:T(128)} %convert_element_type.82, () %tuple.106, (s32[]{:T(128)}, s32[]{:T(128)}, s32[]{:T(128)}, s32[4]{0:T(128)S(1)}, s32[]{:T(128)}, /*index=5*/s32[]{:T(128)}, bf16[4,4,8,224]{3,1,2,0:T(4,128)(2,1)S(1)}, bf16[4,512,1792]{1,2,0:T(8,128)(2,1)}, s32[512]{0:T(512)S(1)}) %tuple.107), branch_computations={%region_5.5_spmd, %region_6.6_spmd} | conditional | flops 7382535 | bytes 5601398 | solution.py:47
  126.4 0.7 broadcast_compare_fusion.1
  127.1 0.6 broadcast_compare_fusion
  127.7 0.7 broadcast_add_fusion.1
  128.4 0.8 fusion.7
  131.1 1.6 constant_dynamic-slice_fusion
  133.1 0.7 dynamic_slice.98
  135.6 0.7 dynamic_slice.99
  136.9 0.7 dynamic_slice.101
  140.3 6.7 %conditional.8 = (f32[1,8,4,512]{3,2,1,0:T(4,128)S(1)}) conditional(s32[]{:T(128)} %convert_element_type.82, () %tuple.106, (s32[]{:T(128)}, s32[]{:T(128)}, s32[]{:T(128)}, s32[4]{0:T(128)S(1)}, s32[]{:T(128)}, /*index=5*/s32[]{:T(128)}, bf16[4,4,8,224]{3,1,2,0:T(4,128)(2,1)S(1)}, bf16[4,512,1792]{1,2,0:T(8,128)(2,1)}, s32[512]{0:T(512)S(1)}) %tuple.107), branch_computations={%region_5.5_spmd, %region_6.6_spmd} | conditional | flops 7382535 | bytes 5601398 | solution.py:47
  140.3 0.7 broadcast_compare_fusion.1
  141.0 0.6 broadcast_compare_fusion
  141.6 0.7 broadcast_add_fusion.1
  142.3 0.8 fusion.7
  145.0 1.6 constant_dynamic-slice_fusion
  147.0 0.7 dynamic_slice.98
  149.6 0.7 dynamic_slice.99
  150.8 0.7 dynamic_slice.101
  154.2 6.7 %conditional.8 = (f32[1,8,4,512]{3,2,1,0:T(4,128)S(1)}) conditional(s32[]{:T(128)} %convert_element_type.82, () %tuple.106, (s32[]{:T(128)}, s32[]{:T(128)}, s32[]{:T(128)}, s32[4]{0:T(128)S(1)}, s32[]{:T(128)}, /*index=5*/s32[]{:T(128)}, bf16[4,4,8,224]{3,1,2,0:T(4,128)(2,1)S(1)}, bf16[4,512,1792]{1,2,0:T(8,128)(2,1)}, s32[512]{0:T(512)S(1)}) %tuple.107), branch_computations={%region_5.5_spmd, %region_6.6_spmd} | conditional | flops 7382535 | bytes 5601398 | solution.py:47
  154.2 0.7 broadcast_compare_fusion.1
  154.9 0.6 broadcast_compare_fusion
  155.6 0.7 broadcast_add_fusion.1
  156.3 0.8 fusion.7
  158.9 1.6 constant_dynamic-slice_fusion
  161.1 33.0 %pmax.7 = f32[4,8,4]{2,1,0:T(8,128)S(1)} all-reduce(f32[4,8,4]{2,1,0:T(8,128)S(1)} %max.5), channel_id=1, replica_groups=mesh['seq'=8,'tensor'=4] {'seq'}, use_global_device_ids=true, to_apply=%region_10.11 | all-reduce | flops 128 | bytes 1024 | tf_op jit(solution)/shard_map/pmax | solution.py:142
  194.2 48.4 %while.30 = (s32[]{:T(128)}, f32[4,8,4]{1,2,0:T(4,128)S(1)}, f32[4,8,4,224]{3,2,1,0:T(4,128)}, s32[4]{0:T(128)S(1)}, s32[4]{0:T(128)S(1)}, /*index=5*/s32[]{:T(1...) while((s32[]{:T(128)}, f32[4,8,4]{1,2,0:T(4,128)S(1)}, ...), condition=%wide.region_15.16_spmd, body=%wide.region_11.15_spmd.sunk | while | flops 7471087 | bytes 5736311 | solution.py:80
  196.7 0.7 dynamic_slice.95
  201.1 4.5 %conditional.7 = (f32[1,8,4]{1,2,0:T(4,128)S(1)}, f32[1,8,4,224]{3,2,1,0:T(4,128)S(1)}) conditional(s32[]{:T(128)} %convert_element_type.81, () %tuple.103, (s32[]{:T(128)}, f32[4,8,4,512]{3,2,1,0:T(4,128)S(1)}, f32[4,8,4]{1,2,0:T(4,128)S(1)}, bf16[4,512,1792]{1,2,0:T(8,128)(2,1)}) %tuple.104), branch_computations={%region_12.12_spmd, %region_13.14_spmd} | conditional | flops 7471075 | bytes 5669954 | solution.py:74
  203.2 1.6 constant_dynamic-slice_fusion.1
  208.8 0.7 dynamic_slice.95
  213.2 4.5 %conditional.7 = (f32[1,8,4]{1,2,0:T(4,128)S(1)}, f32[1,8,4,224]{3,2,1,0:T(4,128)S(1)}) conditional(s32[]{:T(128)} %convert_element_type.81, () %tuple.103, (s32[]{:T(128)}, f32[4,8,4,512]{3,2,1,0:T(4,128)S(1)}, f32[4,8,4]{1,2,0:T(4,128)S(1)}, bf16[4,512,1792]{1,2,0:T(8,128)(2,1)}) %tuple.104), branch_computations={%region_12.12_spmd, %region_13.14_spmd} | conditional | flops 7471075 | bytes 5669954 | solution.py:74
  215.3 1.6 constant_dynamic-slice_fusion.1
  220.9 0.7 dynamic_slice.95
  225.3 4.5 %conditional.7 = (f32[1,8,4]{1,2,0:T(4,128)S(1)}, f32[1,8,4,224]{3,2,1,0:T(4,128)S(1)}) conditional(s32[]{:T(128)} %convert_element_type.81, () %tuple.103, (s32[]{:T(128)}, f32[4,8,4,512]{3,2,1,0:T(4,128)S(1)}, f32[4,8,4]{1,2,0:T(4,128)S(1)}, bf16[4,512,1792]{1,2,0:T(8,128)(2,1)}) %tuple.104), branch_computations={%region_12.12_spmd, %region_13.14_spmd} | conditional | flops 7471075 | bytes 5669954 | solution.py:74
  227.3 1.6 constant_dynamic-slice_fusion.1
  233.0 0.7 dynamic_slice.95
  237.4 4.5 %conditional.7 = (f32[1,8,4]{1,2,0:T(4,128)S(1)}, f32[1,8,4,224]{3,2,1,0:T(4,128)S(1)}) conditional(s32[]{:T(128)} %convert_element_type.81, () %tuple.103, (s32[]{:T(128)}, f32[4,8,4,512]{3,2,1,0:T(4,128)S(1)}, f32[4,8,4]{1,2,0:T(4,128)S(1)}, bf16[4,512,1792]{1,2,0:T(8,128)(2,1)}) %tuple.104), branch_computations={%region_12.12_spmd, %region_13.14_spmd} | conditional | flops 7471075 | bytes 5669954 | solution.py:74
  239.4 1.6 constant_dynamic-slice_fusion.1
  242.7 0.7 pad_maximum_fusion
  243.9 33.1 %psum.46 = f32[4,8,4]{2,1,0:T(8,128)S(1)} all-reduce(f32[4,8,4]{2,1,0:T(8,128)S(1)} %copy.62), channel_id=1, replica_groups=mesh['seq'=8,'tensor'=4] {'seq'}, use_global_device_ids=true, to_apply=%region_17.18 | all-reduce | flops 128 | bytes 1024 | tf_op jit(solution)/shard_map/psum | solution.py:144
  277.0 32.8 %all-reduce.6.cloned.1.call-done = f32[4,8,4,224]{3,2,1,0:T(4,128)} async-done(((f32[4,8,4,224]{3,2,1,0:T(4,128)}), f32[4,8,4,224]{3,2,1,0:T(4,128)}) %all-reduce.6.cloned.1.call-update) | async-done | bytes 114704 | tf_op jit(solution)/shard_map/psum | solution.py:144
  309.8 1.1 fusion.20
  311.5 10.9 %psum.47 = f32[16,448]{1,0:T(8,128)} all-reduce(f32[16,448]{1,0:T(8,128)S(1)} %fusion.39), channel_id=1, replica_groups=mesh['seq'=8,'tensor'=4] {'tensor'}, use_global_device_ids=true, to_apply=%region_19.20 | all-reduce | flops 7168 | bytes 57344 | tf_op jit(solution)/shard_map/psum | solution.py:155
  (104 shorter events, 20.0 us)
Async XLA Ops:
  7.2 303.8 %copy-start = (bf16[1792,448]{0,1:T(8,128)(2,1)S(1)}, bf16[1792,448]{0,1:T(8,128)(2,1)}, u32[]{:S(2)}) copy-start(bf16[1792,448]{0,1:T(8,128)(2,1)} %param.24) | copy-start | bytes 4816900
  7.2 13.5 %copy-start.2 = (bf16[16,896]{1,0:T(8,128)(2,1)S(1)}, bf16[16,896]{1,0:T(8,128)(2,1)}, u32[]{:S(2)}) copy-start(bf16[16,896]{1,0:T(8,128)(2,1)} %param.19) | copy-start | bytes 86020
  7.2 13.5 %copy-start.4 = (f32[896]{0:T(1024)S(1)}, f32[896]{0:T(1024)}, u32[]{:S(2)}) copy-start(f32[896]{0:T(1024)} %param.20) | copy-start | bytes 10756
  7.2 94.9 %all-reduce.4.cloned.1.call-start = ((), (), s32[]{:S(2)}) async-start(), calls=%async_computation | async-start | bytes 688128 | tf_op jit(solution)/shard_map/psum | solution.py:129
  20.6 7.2 %copy-start.3 = (bf16[896,128]{1,0:T(8,128)(2,1)S(1)}, bf16[896,128]{1,0:T(8,128)(2,1)}, u32[]{:S(2)}) copy-start(bf16[896,128]{1,0:T(8,128)(2,1)} %param.22) | copy-start | bytes 688132
  27.8 281.9 %all-reduce.6.cloned.1.call-start = ((), (), s32[]{:S(2)}) async-start(), calls=%async_computation.1 | async-start | bytes 262144 | tf_op jit(solution)/shard_map/psum | solution.py:144
  61.9 41.4 %copy-start.1 = (bf16[128,1792]{1,0:T(8,128)(2,1)S(1)}, bf16[128,1792]{1,0:T(8,128)(2,1)}, u32[]{:S(2)}) copy-start(bf16[128,1792]{1,0:T(8,128)(2,1)} %param.23) | copy-start | bytes 1376260
  71.9 33.3 %copy-start.5 = (s32[4]{0:T(128)S(1)}, s32[4]{0:T(128)}, u32[]{:S(2)}) copy-start(s32[4]{0:T(128)} %param.27) | copy-start | bytes 52
  71.9 33.3 %copy-start.6 = (s32[4]{0:T(128)S(1)}, s32[4]{0:T(128)}, u32[]{:S(2)}) copy-start(s32[4]{0:T(128)} %param.28) | copy-start | bytes 52
  71.9 33.3 %copy-start.7 = (s32[4]{0:T(128)S(1)}, s32[4]{0:T(128)}, u32[]{:S(2)}) copy-start(s32[4]{0:T(128)} %param.29) | copy-start | bytes 52
Sparse Core Ops, SparseCore 0:
  28.0 74.1 all-reduce.3
  242.8 66.9 all-reduce.5
where the time goes:
time: 331 us; the launch traced here: 329 us
  blocking collectives  101 us (31%)
  local copies, waits for them, and re-layouts  71 us (21%)
  waiting for transfers between devices  63 us (19%)
  loops' own time  52.2 us (16%)
  between operations  14.2 us (4%)
  other arithmetic  14.1 us (4%)
  matrix products  13.9 us (4%)
    psum x1, blocking collectives, shards(): total, output = lax.psum((total, output), 'seq')  33.1 us
    pmax x1, blocking collectives, shards(): top = lax.pmax(local_top, 'seq')  33 us
    psum x1, waiting for transfers between devices, shards(): total, output = lax.psum((total, output), 'seq')  32.8 us
    psum x1, waiting for transfers between devices, shards(): projected = lax.psum(partial_proj, 'seq')  30.2 us
    psum x1, blocking collectives, row_stats(): return lax.psum((partial_low_rank, partial_sq), 'seq')  23.7 us
    unnamed x21, local copies, waits for them, and re-layouts  23.6 us
    another operation x1, loops' own time, cache_scores(): return lax.map(score_one, jnp.arange(count, dtype=jnp.int32))  18.6 us
    another operation x1, loops' own time, cache_terms(): return lax.map(weigh_one, jnp.arange(count, dtype=jnp.int32))  18 us
  transfers between devices with their start and end apart: 2, of which 2 were waited for; matrix products, arithmetic and copies ran while one was open for 7% of the time, Pallas kernels for 0%

commit v1 on v0

v1 whole, which is shorter than its diff:
```python
import functools

import jax
import jax.numpy as jnp
from jax import lax
from jax.experimental import pallas as pl
from jax.experimental.pallas import tpu as pltpu
from jax.sharding import PartitionSpec as P

HD = 224
NEW = 4
INPUT_WIDTH = 7168
PAD = 256
SIDE = 16

NEG = -1e30
CUT = -1e29
MESH = pl.DeviceIdType.MESH
F32 = jnp.float32
BF16 = jnp.bfloat16


def dot_t(a, b):
    return lax.dot_general(a, b, (((1,), (1,)), ((), ())), preferred_element_type=F32)


def block_kernel(
    seq, tensor, heads, count,
    x_hbm, g_hbm, w_hbm, down_hbm, up_hbm, wo_hbm, k_hbm, v_hbm, len_ref, sink_ref, win_ref,
    mixed_ref, kv_ref,
    x_v, g_v, w_v, down_v, up_v, wo_v, k_v, v_v,
    q_send, q_part, q_all, q_full, qblk,
    kv_send, kv_part, kv_all,
    o_full, m_full, l_full, o_send, o_part, a_all, a_full, t_part, prob, load_sem,
    q_ss, q_rs, qa_ss, qa_rs, kv_ss, kv_rs, kva_ss, kva_rs, o_ss, o_rs, a_ss, a_rs, t_ss, t_rs,
):
    me = lax.axis_index("seq")
    mine_t = lax.axis_index("tensor")
    per = seq // heads
    my_h = lax.div(me, jnp.int32(per))
    owner = lax.rem(me, jnp.int32(per)) == 0
    span = k_v.shape[1]
    rows = x_v.shape[0]
    group = NEW * heads

    def load(src, dst, index):
        return pltpu.make_async_copy(src, dst, load_sem.at[index])

    first = [load(x_hbm, x_v, 0), load(g_hbm, g_v, 1), load(w_hbm.at[0], w_v.at[0], 2),
             load(down_hbm, down_v, 3), load(up_hbm, up_v, 4)]
    rest = [load(w_hbm.at[1], w_v.at[1], 5), load(w_hbm.at[2], w_v.at[2], 6)]
    keys = [load(k_hbm.at[r], k_v.at[r], 8 + r) for r in range(count)]
    values = [load(v_hbm.at[r], v_v.at[r], 8 + count + r) for r in range(count)]
    wo_load = load(wo_hbm, wo_v, 7)
    for c in first:
        c.start()

    barrier = pltpu.get_barrier_semaphore()
    for d in range(1, seq):
        pl.semaphore_signal(barrier, inc=1, device_id={"seq": lax.rem(me + d, seq)}, device_id_type=MESH)
    for d in range(1, tensor):
        pl.semaphore_signal(barrier, inc=1, device_id={"tensor": lax.rem(mine_t + d, tensor)}, device_id_type=MESH)

    def on_owner(f):
        if per == 1:
            f()
        else:
            pl.when(owner)(f)

    def to_owners(src, dst, ss, rs, act):
        for d in range(1 if per == 1 else 0, heads):
            h = lax.rem(my_h + d, heads)

            def one(h=h, d=d):
                act(pltpu.make_async_remote_copy(
                    src_ref=src.at[h], dst_ref=dst.at[me], send_sem=ss.at[d], recv_sem=rs.at[me],
                    device_id={"seq": h * per}, device_id_type=MESH))

            if per == 1:
                one()
            else:
                pl.when(h * per != me)(one)

    def wait_parts(src, dst, rs, ss):
        for d in range(1, seq):
            s = lax.rem(me + d, seq)
            pltpu.make_async_remote_copy(
                src_ref=src.at[0], dst_ref=dst.at[s], send_sem=ss.at[0], recv_sem=rs.at[s],
                device_id={"seq": s}, device_id_type=MESH).wait_recv()

    def from_owner(buf, ss, rs, act):
        for d in range(1, seq):
            act(pltpu.make_async_remote_copy(
                src_ref=buf.at[my_h], dst_ref=buf.at[my_h], send_sem=ss.at[d], recv_sem=rs.at[my_h],
                device_id={"seq": lax.rem(me + d, seq)}, device_id_type=MESH))

    def wait_results(buf, ss, rs):
        for d in range(1 if per == 1 else 0, heads):
            h = lax.rem(my_h + d, heads)

            def one(h=h):
                pltpu.make_async_remote_copy(
                    src_ref=buf.at[h], dst_ref=buf.at[h], send_sem=ss.at[0], recv_sem=rs.at[h],
                    device_id={"seq": lax.rem(me + 1, seq)}, device_id_type=MESH).wait_recv()

            if per == 1:
                one()
            else:
                pl.when(h * per != me)(one)

    start = lambda c: c.start()
    wait_send = lambda c: c.wait_send()

    def head(h):
        return slice(h * HD, (h + 1) * HD)

    for c in first[:2]:
        c.wait()
    feat = x_v[...].astype(F32)
    scaled = (feat * g_v[...].reshape(1, feat.shape[1])).astype(BF16)
    sq = jnp.sum(feat * feat, axis=1, keepdims=True)
    first[2].wait()
    for c in rest:
        c.start()
    for c in keys:
        c.start()
    first[3].wait()
    first[4].wait()
    low = jnp.dot(scaled, down_v[...], preferred_element_type=F32)
    low_hi = low.astype(BF16)
    low_lo = (low - low_hi.astype(F32)).astype(BF16)
    q_partial = jnp.dot(scaled, w_v[0], preferred_element_type=F32)
    q_partial += jnp.dot(low_hi, up_v[...], preferred_element_type=F32)
    q_partial += jnp.dot(low_lo, up_v[...], preferred_element_type=F32)
    for h in range(heads):
        q_send[h, :, 0:HD] = q_partial[:, head(h)]
        q_send[h, :, HD:PAD] = jnp.broadcast_to(sq, (rows, PAD - HD))
    pl.semaphore_wait(barrier, seq + tensor - 2)
    to_owners(q_send, q_part, q_ss, q_rs, start)

    for c in values:
        c.start()
    wo_load.start()
    for j in range(2):
        rest[j].wait()
        part = jnp.dot(scaled, w_v[1 + j], preferred_element_type=F32)
        for h in range(heads):
            kv_send[h, j, :, 0:HD] = part[:, head(h)]
            kv_send[h, j, :, HD:PAD] = jnp.zeros((rows, PAD - HD), F32)

    def scale_of(total):
        return lax.rsqrt(total[:, HD:HD + 1] / INPUT_WIDTH + 1e-05)

    def sum_queries():
        q_part[me] = q_send[my_h]
        wait_parts(q_send, q_part, q_rs, q_ss)
        total = q_part[0]
        for s in range(1, seq):
            total = total + q_part[s]
        scale = scale_of(total)
        lane = lax.broadcasted_iota(jnp.int32, (rows, PAD), 1)
        q_all[my_h] = jnp.where(lane < HD, total * scale, scale)
        from_owner(q_all, qa_ss, qa_rs, start)

    on_owner(sum_queries)
    to_owners(kv_send, kv_part, kv_ss, kv_rs, start)
    wait_results(q_all, qa_ss, qa_rs)
    for h in range(heads):
        q_full[:, head(h)] = q_all[h, :, 0:HD]

    row = lax.broadcasted_iota(jnp.int32, (group, heads * HD), 0)
    col = lax.broadcasted_iota(jnp.int32, (group, heads * HD), 1)
    low_col = lax.div(row, jnp.int32(NEW)) * HD
    own_head = (col >= low_col) & (col < low_col + HD)

    def fold(full):
        kept = jnp.where(own_head, full, 0.0)
        eight = kept[0:8]
        for i in range(1, group // 8):
            eight = eight + kept[8 * i:8 * i + 8]
        return eight[0:NEW] + eight[NEW:2 * NEW]

    s_row = lax.rem(lax.broadcasted_iota(jnp.int32, (group, span), 0), jnp.int32(NEW))
    position = me * span + lax.broadcasted_iota(jnp.int32, (group, span), 1)
    width = heads * HD
    for r in range(count):
        four = q_full[NEW * r:NEW * (r + 1), :]
        eight = jnp.concatenate([four, four], axis=0)
        tall = jnp.concatenate([eight] * (group // 8), axis=0)
        qblk[r] = jnp.where(own_head, tall, 0.0).astype(BF16)
        keys[r].wait()
        raw = dot_t(qblk[r], k_v[r]) * HD ** (-0.5)
        length = len_ref[r]
        seen = (position < length) & (
            (position < sink_ref[r]) | (length + s_row - position < win_ref[r]))
        scores = jnp.where(seen, raw, NEG)
        top = jnp.max(scores, axis=1, keepdims=True)
        expo = jnp.where(seen, jnp.exp(scores - top), 0.0)
        total = jnp.sum(expo, axis=1, keepdims=True)
        prob[r] = expo.astype(BF16)
        m_full[NEW * r:NEW * (r + 1), :] = fold(jnp.broadcast_to(top, (group, width)))
        l_full[NEW * r:NEW * (r + 1), :] = fold(jnp.broadcast_to(total, (group, width)))

    def sum_new():
        kv_part[me] = kv_send[my_h]
        wait_parts(kv_send, kv_part, kv_rs, kv_ss)
        scale = q_all[my_h][:, HD:HD + 1]
        for j in range(2):
            total = kv_part[0, j]
            for s in range(1, seq):
                total = total + kv_part[s, j]
            kv_all[my_h, j] = total * scale
        from_owner(kv_all, kva_ss, kva_rs, start)

    on_owner(sum_new)

    for r in range(count):
        values[r].wait()
        out = jnp.dot(prob[r], v_v[r], preferred_element_type=F32)
        o_full[NEW * r:NEW * (r + 1), :] = fold(out)
    for h in range(heads):
        o_send[h, :, 0:HD] = o_full[:, head(h)]
        o_send[h, :, HD:HD + SIDE] = m_full[:, h * HD:h * HD + SIDE]
        o_send[h, :, HD + SIDE:PAD] = l_full[:, h * HD:h * HD + SIDE]
    to_owners(o_send, o_part, o_ss, o_rs, start)

    def merge():
        query = q_all[my_h][:, 0:HD].astype(BF16)
        key = kv_all[my_h, 0][:, 0:HD].astype(BF16)
        value = kv_all[my_h, 1][:, 0:HD].astype(BF16)
        token = lax.broadcasted_iota(jnp.int32, (rows, rows), 0)
        other = lax.broadcasted_iota(jnp.int32, (rows, rows), 1)
        seen = (lax.div(token, jnp.int32(NEW)) == lax.div(other, jnp.int32(NEW))) & (other <= token)
        fresh = jnp.where(seen, dot_t(query, key) * HD ** (-0.5), NEG)
        own_top = jnp.max(fresh, axis=1, keepdims=True)
        expo = jnp.where(seen, jnp.exp(fresh - own_top), 0.0)
        own_sum = jnp.sum(expo, axis=1, keepdims=True)
        own_out = jnp.dot(expo.astype(BF16), value, preferred_element_type=F32)
        o_part[me] = o_send[my_h]
        wait_parts(o_send, o_part, o_rs, o_ss)
        top = own_top
        for s in range(seq):
            top = jnp.maximum(top, o_part[s][:, HD:HD + 1])
        factor = jnp.exp(own_top - top)
        total = own_sum * factor
        out = own_out * factor
        for s in range(seq):
            piece = o_part[s]
            factor = jnp.exp(piece[:, HD:HD + 1] - top)
            out = out + piece[:, 0:HD] * factor
            total = total + piece[:, HD + SIDE:HD + SIDE + 1] * factor
        a_all[my_h, :, 0:HD] = out / total
        a_all[my_h, :, HD:PAD] = jnp.zeros((rows, PAD - HD), F32)
        from_owner(a_all, a_ss, a_rs, start)

    on_owner(merge)

    wait_results(kv_all, kva_ss, kva_rs)
    for h in range(heads):
        for j in range(2):
            kv_ref[j, :, head(h)] = kv_all[h, j, :, 0:HD]
    wo_load.wait()
    wait_results(a_all, a_ss, a_rs)
    for h in range(heads):
        a_full[:, head(h)] = a_all[h, :, 0:HD]
    t_part[mine_t] = dot_t(a_full[...].astype(BF16), wo_v[...])

    def to_tensor(d):
        return pltpu.make_async_remote_copy(
            src_ref=t_part.at[mine_t], dst_ref=t_part.at[mine_t], send_sem=t_ss.at[d],
            recv_sem=t_rs.at[mine_t], device_id={"tensor": lax.rem(mine_t + d, tensor)},
            device_id_type=MESH)

    for d in range(1, tensor):
        to_tensor(d).start()
    to_owners(q_send, q_part, q_ss, q_rs, wait_send)
    to_owners(kv_send, kv_part, kv_ss, kv_rs, wait_send)
    to_owners(o_send, o_part, o_ss, o_rs, wait_send)
    on_owner(lambda: from_owner(q_all, qa_ss, qa_rs, wait_send))
    on_owner(lambda: from_owner(kv_all, kva_ss, kva_rs, wait_send))
    on_owner(lambda: from_owner(a_all, a_ss, a_rs, wait_send))
    for d in range(1, tensor):
        s = lax.rem(mine_t + d, tensor)
        pltpu.make_async_remote_copy(
            src_ref=t_part.at[s], dst_ref=t_part.at[s], send_sem=t_ss.at[0], recv_sem=t_rs.at[s],
            device_id={"tensor": s}, device_id_type=MESH).wait_recv()
    mixed = t_part[0]
    for s in range(1, tensor):
        mixed = mixed + t_part[s]
    mixed_ref[...] = mixed
    for d in range(1, tensor):
        to_tensor(d).wait_send()


def shards(
    seq, tensor,
    features, input_norm_scale, query_key_value_weight, adapter_down_weight, adapter_up_weight,
    output_weight, cached_key_rows, cached_value_rows, lengths, sinks, windows,
):
    rows, depth = features.shape
    count, span, width = cached_key_rows.shape
    heads = width // HD
    out_width = output_weight.shape[1]
    group = NEW * heads
    weights = jnp.transpose(query_key_value_weight, (1, 0, 2))
    wo = jnp.transpose(output_weight)
    hbm = pl.BlockSpec(memory_space=pltpu.HBM)
    smem = pl.BlockSpec(memory_space=pltpu.SMEM)
    vmem = pl.BlockSpec(memory_space=pltpu.VMEM)

    def like(a):
        return pltpu.VMEM(a.shape, a.dtype)

    dma = lambda n: pltpu.SemaphoreType.DMA((n,))
    ring = max(seq, heads)
    return pl.pallas_call(
        functools.partial(block_kernel, seq, tensor, heads, count),
        out_shape=(
            jax.ShapeDtypeStruct((rows, out_width), F32),
            jax.ShapeDtypeStruct((2, rows, width), F32),
        ),
        in_specs=[hbm] * 8 + [smem] * 3,
        out_specs=(vmem, vmem),
        scratch_shapes=[
            like(features), like(input_norm_scale), like(weights), like(adapter_down_weight),
            like(adapter_up_weight), like(wo), like(cached_key_rows), like(cached_value_rows),
            pltpu.VMEM((heads, rows, PAD), F32),
            pltpu.VMEM((seq, rows, PAD), F32),
            pltpu.VMEM((heads, rows, PAD), F32),
            pltpu.VMEM((rows, width), F32),
            pltpu.VMEM((count, group, width), BF16),
            pltpu.VMEM((heads, 2, rows, PAD), F32),
            pltpu.VMEM((seq, 2, rows, PAD), F32),
            pltpu.VMEM((heads, 2, rows, PAD), F32),
            pltpu.VMEM((rows, width), F32),
            pltpu.VMEM((rows, width), F32),
            pltpu.VMEM((rows, width), F32),
            pltpu.VMEM((heads, rows, PAD), F32),
            pltpu.VMEM((seq, rows, PAD), F32),
            pltpu.VMEM((heads, rows, PAD), F32),
            pltpu.VMEM((rows, width), F32),
            pltpu.VMEM((tensor, rows, out_width), F32),
            pltpu.VMEM((count, group, span), BF16),
            dma(8 + 2 * count),
        ] + [dma(ring)] * 12 + [dma(tensor)] * 2,
        compiler_params=pltpu.CompilerParams(
            collective_id=0, has_side_effects=True, vmem_limit_bytes=60 * 1024 * 1024,
        ),
    )(
        features, input_norm_scale, weights, adapter_down_weight, adapter_up_weight, wo,
        cached_key_rows, cached_value_rows, lengths, sinks, windows,
    )


def solution(mesh):
    in_specs = (
        P(None, "seq"),
        P("seq"),
        P("seq", None, "tensor"),
        P("seq", None),
        P(None, "tensor"),
        P("tensor", "seq"),
        P(None, "seq", "tensor"),
        P(None, "seq", "tensor"),
        P(),
        P(),
        P(),
    )
    out_specs = (P(None, "seq"), P(None, None, "tensor"))
    body = functools.partial(shards, mesh.shape["seq"], mesh.shape["tensor"])
    return jax.shard_map(body, mesh=mesh, in_specs=in_specs, out_specs=out_specs, check_vma=False)
```

time: 331 us -> 45.3 us (0.14)
  blocking collectives: 101 us -> 0 us
  local copies, waits for them, and re-layouts: 71 us -> 3.02 us
  waiting for transfers between devices: 63 us -> 0 us
  loops' own time: 52.2 us -> 0 us
  Pallas kernels: 0 us -> 41.4 us
  other arithmetic: 14.1 us -> 0 us
  matrix products: 13.9 us -> 0 us
  between operations: 14.2 us -> 0.64 us
    psum x3 -> x0, blocking collectives: 67.6 us -> none  [the longest x1 33.1 us: shards(): total, output = lax.psum((total, output), 'seq')]
    psum x2 -> x0, waiting for transfers between devices: 63 us -> none  [the longest x1 32.8 us: shards(): total, output = lax.psum((total, output), 'seq')]
    another operation x10 -> x0, loops' own time: 52.2 us -> none  [the longest x1 18.6 us: cache_scores(): return lax.map(score_one, jnp.arange(count, dtype=jnp.int32))]
    pallas_call x0 -> x1, Pallas kernels: none -> 41.4 us  [shards(): pl.pallas_call(functools.partial(block_kernel, seq, tensor, heads, count)...]
    dynamic_slice x40 -> x0, local copies, waits for them, and re-layouts: 33 us -> none  [the longest x4 6.49 us: score_compute(): keys = cached_key_rows[index].reshape(span, heads, HD)]
    pmax x1 -> x0, blocking collectives: 33 us -> none  [shards(): top = lax.pmax(local_top, 'seq')]
    unnamed x21 -> x2, local copies, waits for them, and re-layouts: 23.6 us -> 3.02 us
    dot_general x14 -> x0, matrix products: 13.9 us -> none  [the longest x1 7.16 us: shards(): jnp.dot(scaled_scores, weights, preferred_element_type=jnp.float32)]
  transfers between devices with their start and end apart: 2 -> 0, of which waited for: 2 -> 0; matrix products, arithmetic and copies ran while one was open for 7% -> 0% of each run, Pallas kernels for 0% -> 0%
where the time goes in v1:
time: 45.3 us; the launch traced here: 45.1 us
  Pallas kernels  41.4 us (91%)
  local copies, waits for them, and re-layouts  3.02 us (7%)
  between operations  0.64 us (1%)
    pallas_call x1, Pallas kernels, shards(): pl.pallas_call(functools.partial(block_kernel, seq, tensor, heads, count)...  41.4 us
    unnamed x2, local copies, waits for them, and re-layouts  3.02 us

profile of v1, /device:TPU:0, one launch (start us, length us, event | category | flops | bytes accessed | tf_op | source)
XLA Modules:
  0.0 45.1 jit_solution(14610729491527650935)
XLA Ops:
  0.6 41.4 %shard_map.122 = (f32[16,448]{1,0:T(8,128)}, f32[2,16,1792]{2,1,0:T(8,128)}) custom-call(bf16[16,896]{1,0:T(8,128)(2,1)} %x_hbm.1, f32[896]{0:T(1024)} %g_hbm.1, bf16[3,896,1792]{2,1,0:T(8,128)(2,1)} %bitcast.2, bf16[896,128]{1,0:T(8,128)(2,1)} %down_hbm.1, bf16[128,1792]{1,0:T(8,128)(2,1)} %up_hbm.1, bf16[448,1792]{1,0:T(8,128)(2,1)} %bitcast.3, ...), custom_call_target="tpu_custom_call" | custom-call | tf_op jit(solution)/shard_map/pallas_call | solution.py:316
  42.0 1.4 %copy.15 = f32[16,448]{1,0:T(8,128)} copy(f32[16,448]{1,0:T(8,128)} %get-tuple-element.4) | data formatting | bytes 57344
  43.4 1.6 %copy.16 = f32[2,16,1792]{2,1,0:T(8,128)} copy(f32[2,16,1792]{2,1,0:T(8,128)} %get-tuple-element.5) | data formatting | bytes 458752

commit v2 on v1

--- a/solution.py
+++ b/solution.py
@@ -26,13 +26,14 @@
 
 def block_kernel(
     seq, tensor, heads, count,
-    x_hbm, g_hbm, w_hbm, down_hbm, up_hbm, wo_hbm, k_hbm, v_hbm, len_ref, sink_ref, win_ref,
+    x_hbm, g_hbm, w_hbm, down_hbm, up_hbm, wo_hbm, k_hbm, v_hbm, len_hbm, sink_hbm, win_hbm,
     mixed_ref, kv_ref,
+    len_ref, sink_ref, win_ref,
     x_v, g_v, w_v, down_v, up_v, wo_v, k_v, v_v,
     q_send, q_part, q_all, q_full, qblk,
-    kv_send, kv_part, kv_all,
+    kv_send, kv_mid, kv_sum, kv_part, kv_all,
     o_full, m_full, l_full, o_send, o_part, a_all, a_full, t_part, prob, load_sem,
-    q_ss, q_rs, qa_ss, qa_rs, kv_ss, kv_rs, kva_ss, kva_rs, o_ss, o_rs, a_ss, a_rs, t_ss, t_rs,
+    q_ss, q_rs, qa_ss, qa_rs, kvm_ss, kvm_rs, kv_ss, kv_rs, kva_ss, kva_rs, o_ss, o_rs, a_ss, a_rs, t_ss, t_rs,
 ):
     me = lax.axis_index("seq")
     mine_t = lax.axis_index("tensor")
@@ -52,7 +53,9 @@
     keys = [load(k_hbm.at[r], k_v.at[r], 8 + r) for r in range(count)]
     values = [load(v_hbm.at[r], v_v.at[r], 8 + count + r) for r in range(count)]
     wo_load = load(wo_hbm, wo_v, 7)
-    for c in first:
+    places = [load(a, b, 8 + 2 * count + i) for i, (a, b) in enumerate(
+        ((len_hbm, len_ref), (sink_hbm, sink_ref), (win_hbm, win_ref)))]
+    for c in first + places:
         c.start()
 
     barrier = pltpu.get_barrier_semaphore()
@@ -141,12 +144,20 @@
     for c in values:
         c.start()
     wo_load.start()
+    paired = per == 1 and seq % 2 == 0
+    half = heads // 2
+    side = lax.rem(me, jnp.int32(2))
+    partner = me + 1 - 2 * side
+
+    def place(h):
+        return h % 2 * half + h // 2 if paired else h
+
     for j in range(2):
         rest[j].wait()
         part = jnp.dot(scaled, w_v[1 + j], preferred_element_type=F32)
         for h in range(heads):
-            kv_send[h, j, :, 0:HD] = part[:, head(h)]
-            kv_send[h, j, :, HD:PAD] = jnp.zeros((rows, PAD - HD), F32)
+            kv_send[place(h), j, :, 0:HD] = part[:, head(h)]
+            kv_send[place(h), j, :, HD:PAD] = jnp.zeros((rows, PAD - HD), F32)
 
     def scale_of(total):
         return lax.rsqrt(total[:, HD:HD + 1] / INPUT_WIDTH + 1e-05)
@@ -163,7 +174,42 @@
         from_owner(q_all, qa_ss, qa_rs, start)
 
     on_owner(sum_queries)
-    to_owners(kv_send, kv_part, kv_ss, kv_rs, start)
+
+    def pair_parts():
+        return pltpu.make_async_remote_copy(
+            src_ref=kv_send.at[pl.ds((1 - side) * half, half)], dst_ref=kv_mid,
+            send_sem=kvm_ss.at[0], recv_sem=kvm_rs.at[0],
+            device_id={"seq": partner}, device_id_type=MESH)
+
+    def pair_sums(d):
+        owner_at = lax.rem(me + 2 * d, seq)
+        return pltpu.make_async_remote_copy(
+            src_ref=kv_sum.at[lax.div(owner_at, jnp.int32(2))],
+            dst_ref=kv_part.at[lax.div(me, jnp.int32(2))],
+            send_sem=kv_ss.at[d], recv_sem=kv_rs.at[lax.div(me, jnp.int32(2))],
+            device_id={"seq": owner_at}, device_id_type=MESH)
+
+    def spread(d):
+        to = partner if d == 0 else lax.rem(me + 2 * d, seq)
+        return pltpu.make_async_remote_copy(
+            src_ref=kv_all.at[me], dst_ref=kv_all.at[me], send_sem=kva_ss.at[d],
+            recv_sem=kva_rs.at[me], device_id={"seq": to}, device_id_type=MESH)
+
+    def forward(d):
+        h = lax.rem(me + 2 * d, seq)
+        return pltpu.make_async_remote_copy(
+            src_ref=kv_all.at[h], dst_ref=kv_all.at[h], send_sem=kva_ss.at[half + d - 1],
+            recv_sem=kva_rs.at[h], device_id={"seq": partner}, device_id_type=MESH)
+
+    def arrived(h):
+        pltpu.make_async_remote_copy(
+            src_ref=kv_all.at[h], dst_ref=kv_all.at[h], send_sem=kva_ss.at[0],
+            recv_sem=kva_rs.at[h], device_id={"seq": partner}, device_id_type=MESH).wait_recv()
+
+    if paired:
+        pair_parts().start()
+    else:
+        to_owners(kv_send, kv_part, kv_ss, kv_rs, start)
     wait_results(q_all, qa_ss, qa_rs)
     for h in range(heads):
         q_full[:, head(h)] = q_all[h, :, 0:HD]
@@ -188,6 +234,9 @@
         eight = jnp.concatenate([four, four], axis=0)
         tall = jnp.concatenate([eight] * (group // 8), axis=0)
         qblk[r] = jnp.where(own_head, tall, 0.0).astype(BF16)
+        if r == 0:
+            for c in places:
+                c.wait()
         keys[r].wait()
         raw = dot_t(qblk[r], k_v[r]) * HD ** (-0.5)
         length = len_ref[r]
@@ -200,17 +249,36 @@
         prob[r] = expo.astype(BF16)
         m_full[NEW * r:NEW * (r + 1), :] = fold(jnp.broadcast_to(top, (group, width)))
         l_full[NEW * r:NEW * (r + 1), :] = fold(jnp.broadcast_to(total, (group, width)))
+        if paired and r == 0:
+            pair_parts().wait_recv()
+            for i in range(half):
+                kv_sum[i] = kv_mid[i] + kv_send[side * half + i]
+            for d in range(1, half):
+                pair_sums(d).start()
 
     def sum_new():
-        kv_part[me] = kv_send[my_h]
-        wait_parts(kv_send, kv_part, kv_rs, kv_ss)
+        if paired:
+            kv_part[lax.div(me, jnp.int32(2))] = kv_sum[lax.div(me, jnp.int32(2))]
+            for d in range(1, half):
+                s = lax.div(lax.rem(me + 2 * d, seq), jnp.int32(2))
+                pltpu.make_async_remote_copy(
+                    src_ref=kv_sum.at[0], dst_ref=kv_part.at[s], send_sem=kv_ss.at[0],
+                    recv_sem=kv_rs.at[s], device_id={"seq": partner},
+                    device_id_type=MESH).wait_recv()
+        else:
+            kv_part[me] = kv_send[my_h]
+            wait_parts(kv_send, kv_part, kv_rs, kv_ss)
         scale = q_all[my_h][:, HD:HD + 1]
         for j in range(2):
             total = kv_part[0, j]
-            for s in range(1, seq):
+            for s in range(1, half if paired else seq):
                 total = total + kv_part[s, j]
             kv_all[my_h, j] = total * scale
-        from_owner(kv_all, kva_ss, kva_rs, start)
+        if paired:
+            for d in range(half):
+                spread(d).start()
+        else:
+            from_owner(kv_all, kva_ss, kva_rs, start)
 
     on_owner(sum_new)
 
@@ -223,6 +291,10 @@
         o_send[h, :, HD:HD + SIDE] = m_full[:, h * HD:h * HD + SIDE]
         o_send[h, :, HD + SIDE:PAD] = l_full[:, h * HD:h * HD + SIDE]
     to_owners(o_send, o_part, o_ss, o_rs, start)
+    if paired:
+        for d in range(1, half):
+            arrived(lax.rem(me + 2 * d, seq))
+            forward(d).start()
 
     def merge():
         query = q_all[my_h][:, 0:HD].astype(BF16)
@@ -255,7 +327,11 @@
 
     on_owner(merge)
 
-    wait_results(kv_all, kva_ss, kva_rs)
+    if paired:
+        for d in range(half):
+            arrived(lax.rem(partner + 2 * d, seq))
+    else:
+        wait_results(kv_all, kva_ss, kva_rs)
     for h in range(heads):
         for j in range(2):
             kv_ref[j, :, head(h)] = kv_all[h, j, :, 0:HD]
@@ -274,10 +350,18 @@
     for d in range(1, tensor):
         to_tensor(d).start()
     to_owners(q_send, q_part, q_ss, q_rs, wait_send)
-    to_owners(kv_send, kv_part, kv_ss, kv_rs, wait_send)
     to_owners(o_send, o_part, o_ss, o_rs, wait_send)
     on_owner(lambda: from_owner(q_all, qa_ss, qa_rs, wait_send))
-    on_owner(lambda: from_owner(kv_all, kva_ss, kva_rs, wait_send))
+    if paired:
+        pair_parts().wait_send()
+        for d in range(1, half):
+            pair_sums(d).wait_send()
+            forward(d).wait_send()
+        for d in range(half):
+            spread(d).wait_send()
+    else:
+        to_owners(kv_send, kv_part, kv_ss, kv_rs, wait_send)
+        on_owner(lambda: from_owner(kv_all, kva_ss, kva_rs, wait_send))
     on_owner(lambda: from_owner(a_all, a_ss, a_rs, wait_send))
     for d in range(1, tensor):
         s = lax.rem(mine_t + d, tensor)
@@ -305,7 +389,6 @@
     weights = jnp.transpose(query_key_value_weight, (1, 0, 2))
     wo = jnp.transpose(output_weight)
     hbm = pl.BlockSpec(memory_space=pltpu.HBM)
-    smem = pl.BlockSpec(memory_space=pltpu.SMEM)
     vmem = pl.BlockSpec(memory_space=pltpu.VMEM)
 
     def like(a):
@@ -319,9 +402,9 @@
             jax.ShapeDtypeStruct((rows, out_width), F32),
             jax.ShapeDtypeStruct((2, rows, width), F32),
         ),
-        in_specs=[hbm] * 8 + [smem] * 3,
+        in_specs=[hbm] * 11,
         out_specs=(vmem, vmem),
-        scratch_shapes=[
+        scratch_shapes=[pltpu.SMEM((count,), jnp.int32)] * 3 + [
             like(features), like(input_norm_scale), like(weights), like(adapter_down_weight),
             like(adapter_up_weight), like(wo), like(cached_key_rows), like(cached_value_rows),
             pltpu.VMEM((heads, rows, PAD), F32),
@@ -330,6 +413,8 @@
             pltpu.VMEM((rows, width), F32),
             pltpu.VMEM((count, group, width), BF16),
             pltpu.VMEM((heads, 2, rows, PAD), F32),
+            pltpu.VMEM((heads // 2, 2, rows, PAD), F32),
+            pltpu.VMEM((heads // 2, 2, rows, PAD), F32),
             pltpu.VMEM((seq, 2, rows, PAD), F32),
             pltpu.VMEM((heads, 2, rows, PAD), F32),
             pltpu.VMEM((rows, width), F32),
@@ -341,8 +426,8 @@
             pltpu.VMEM((rows, width), F32),
             pltpu.VMEM((tensor, rows, out_width), F32),
             pltpu.VMEM((count, group, span), BF16),
-            dma(8 + 2 * count),
-        ] + [dma(ring)] * 12 + [dma(tensor)] * 2,
+            dma(11 + 2 * count),
+        ] + [dma(ring)] * 4 + [dma(1)] * 2 + [dma(ring)] * 8 + [dma(tensor)] * 2,
         compiler_params=pltpu.CompilerParams(
             collective_id=0, has_side_effects=True, vmem_limit_bytes=60 * 1024 * 1024,
         ),

time: 45.3 us -> 42.7 us (0.943)
  Pallas kernels: 41.4 us -> 38.9 us
    pallas_call x1, Pallas kernels: 41.4 us -> 38.9 us  [shards(): pl.pallas_call(functools.partial(block_kernel, seq, tensor, heads, count)...]
where the time goes in v2:
time: 42.7 us; the launch traced here: 42.5 us
  Pallas kernels  38.9 us (91%)
  local copies, waits for them, and re-layouts  3.02 us (7%)
  between operations  0.64 us (1%)
    pallas_call x1, Pallas kernels, shards(): pl.pallas_call(functools.partial(block_kernel, seq, tensor, heads, count)...  38.9 us
    unnamed x2, local copies, waits for them, and re-layouts  3.02 us

profile of v2, /device:TPU:0, one launch (start us, length us, event | category | flops | bytes accessed | tf_op | source)
XLA Modules:
  0.0 42.5 jit_solution(10554695428471170725)
XLA Ops:
  0.6 38.9 %shard_map.122 = (f32[16,448]{1,0:T(8,128)}, f32[2,16,1792]{2,1,0:T(8,128)}) custom-call(bf16[16,896]{1,0:T(8,128)(2,1)} %x_hbm.1, f32[896]{0:T(1024)} %g_hbm.1, bf16[3,896,1792]{2,1,0:T(8,128)(2,1)} %bitcast.2, bf16[896,128]{1,0:T(8,128)(2,1)} %down_hbm.1, bf16[128,1792]{1,0:T(8,128)(2,1)} %up_hbm.1, bf16[448,1792]{1,0:T(8,128)(2,1)} %bitcast.3, ...), custom_call_target="tpu_custom_call" | custom-call | tf_op jit(solution)/shard_map/pallas_call | solution.py:399
  39.5 1.4 %copy.15 = f32[16,448]{1,0:T(8,128)} copy(f32[16,448]{1,0:T(8,128)} %get-tuple-element.4) | data formatting | bytes 57344
  40.9 1.6 %copy.16 = f32[2,16,1792]{2,1,0:T(8,128)} copy(f32[2,16,1792]{2,1,0:T(8,128)} %get-tuple-element.5) | data formatting | bytes 458752

commit v3 on v2

--- a/solution.py
+++ b/solution.py
@@ -30,9 +30,9 @@
     mixed_ref, kv_ref,
     len_ref, sink_ref, win_ref,
     x_v, g_v, w_v, down_v, up_v, wo_v, k_v, v_v,
-    q_send, q_part, q_all, q_full, qblk,
+    q_send, q_part, q_all, q_full,
     kv_send, kv_mid, kv_sum, kv_part, kv_all,
-    o_full, m_full, l_full, o_send, o_part, a_all, a_full, t_part, prob, load_sem,
+    o_send, o_part, a_all, a_full, t_part, load_sem,
     q_ss, q_rs, qa_ss, qa_rs, kvm_ss, kvm_rs, kv_ss, kv_rs, kva_ss, kva_rs, o_ss, o_rs, a_ss, a_rs, t_ss, t_rs,
 ):
     me = lax.axis_index("seq")
@@ -43,6 +43,8 @@
     span = k_v.shape[1]
     rows = x_v.shape[0]
     group = NEW * heads
+    halves = rows // 8
+    each = count // halves
 
     def load(src, dst, index):
         return pltpu.make_async_copy(src, dst, load_sem.at[index])
@@ -70,13 +72,22 @@
         else:
             pl.when(owner)(f)
 
-    def to_owners(src, dst, ss, rs, act):
+    ring = max(seq, heads)
+
+    def view(ref, index, g):
+        return ref.at[index] if g is None else ref.at[index, pl.ds(8 * g, 8)]
+
+    def slot(index, g):
+        return index if g is None else g * ring + index
+
+    def to_owners(src, dst, ss, rs, act, g=None):
         for d in range(1 if per == 1 else 0, heads):
             h = lax.rem(my_h + d, heads)
 
             def one(h=h, d=d):
                 act(pltpu.make_async_remote_copy(
-                    src_ref=src.at[h], dst_ref=dst.at[me], send_sem=ss.at[d], recv_sem=rs.at[me],
+                    src_ref=view(src, h, g), dst_ref=view(dst, me, g),
+                    send_sem=ss.at[slot(d, g)], recv_sem=rs.at[slot(me, g)],
                     device_id={"seq": h * per}, device_id_type=MESH))
 
             if per == 1:
@@ -84,26 +95,29 @@
             else:
                 pl.when(h * per != me)(one)
 
-    def wait_parts(src, dst, rs, ss):
+    def wait_parts(src, dst, rs, ss, g=None):
         for d in range(1, seq):
             s = lax.rem(me + d, seq)
             pltpu.make_async_remote_copy(
-                src_ref=src.at[0], dst_ref=dst.at[s], send_sem=ss.at[0], recv_sem=rs.at[s],
+                src_ref=view(src, 0, g), dst_ref=view(dst, s, g),
+                send_sem=ss.at[0], recv_sem=rs.at[slot(s, g)],
                 device_id={"seq": s}, device_id_type=MESH).wait_recv()
 
-    def from_owner(buf, ss, rs, act):
+    def from_owner(buf, ss, rs, act, g=None):
         for d in range(1, seq):
             act(pltpu.make_async_remote_copy(
-                src_ref=buf.at[my_h], dst_ref=buf.at[my_h], send_sem=ss.at[d], recv_sem=rs.at[my_h],
+                src_ref=view(buf, my_h, g), dst_ref=view(buf, my_h, g),
+                send_sem=ss.at[slot(d, g)], recv_sem=rs.at[slot(my_h, g)],
                 device_id={"seq": lax.rem(me + d, seq)}, device_id_type=MESH))
 
-    def wait_results(buf, ss, rs):
+    def wait_results(buf, ss, rs, g=None):
         for d in range(1 if per == 1 else 0, heads):
             h = lax.rem(my_h + d, heads)
 
             def one(h=h):
                 pltpu.make_async_remote_copy(
-                    src_ref=buf.at[h], dst_ref=buf.at[h], send_sem=ss.at[0], recv_sem=rs.at[h],
+                    src_ref=view(buf, h, g), dst_ref=view(buf, h, g),
+                    send_sem=ss.at[0], recv_sem=rs.at[slot(h, g)],
                     device_id={"seq": lax.rem(me + 1, seq)}, device_id_type=MESH).wait_recv()
 
             if per == 1:
@@ -139,7 +153,8 @@
         q_send[h, :, 0:HD] = q_partial[:, head(h)]
         q_send[h, :, HD:PAD] = jnp.broadcast_to(sq, (rows, PAD - HD))
     pl.semaphore_wait(barrier, seq + tensor - 2)
-    to_owners(q_send, q_part, q_ss, q_rs, start)
+    for g in range(halves):
+        to_owners(q_send, q_part, q_ss, q_rs, start, g)
 
     for c in values:
         c.start()
@@ -162,18 +177,20 @@
     def scale_of(total):
         return lax.rsqrt(total[:, HD:HD + 1] / INPUT_WIDTH + 1e-05)
 
-    def sum_queries():
-        q_part[me] = q_send[my_h]
-        wait_parts(q_send, q_part, q_rs, q_ss)
-        total = q_part[0]
+    def sum_queries(g):
+        at = slice(8 * g, 8 * g + 8)
+        q_part[me, at] = q_send[my_h, at]
+        wait_parts(q_send, q_part, q_rs, q_ss, g)
+        total = q_part[0, at]
         for s in range(1, seq):
-            total = total + q_part[s]
+            total = total + q_part[s, at]
         scale = scale_of(total)
-        lane = lax.broadcasted_iota(jnp.int32, (rows, PAD), 1)
-        q_all[my_h] = jnp.where(lane < HD, total * scale, scale)
-        from_owner(q_all, qa_ss, qa_rs, start)
-
-    on_owner(sum_queries)
+        lane = lax.broadcasted_iota(jnp.int32, (8, PAD), 1)
+        q_all[my_h, at] = jnp.where(lane < HD, total * scale, scale)
+        from_owner(q_all, qa_ss, qa_rs, start, g)
+
+    for g in range(halves):
+        on_owner(functools.partial(sum_queries, g))
 
     def pair_parts():
         return pltpu.make_async_remote_copy(
@@ -210,9 +227,6 @@
         pair_parts().start()
     else:
         to_owners(kv_send, kv_part, kv_ss, kv_rs, start)
-    wait_results(q_all, qa_ss, qa_rs)
-    for h in range(heads):
-        q_full[:, head(h)] = q_all[h, :, 0:HD]
 
     row = lax.broadcasted_iota(jnp.int32, (group, heads * HD), 0)
     col = lax.broadcasted_iota(jnp.int32, (group, heads * HD), 1)
@@ -229,16 +243,14 @@
     s_row = lax.rem(lax.broadcasted_iota(jnp.int32, (group, span), 0), jnp.int32(NEW))
     position = me * span + lax.broadcasted_iota(jnp.int32, (group, span), 1)
     width = heads * HD
-    for r in range(count):
+
+    def weigh(r):
         four = q_full[NEW * r:NEW * (r + 1), :]
         eight = jnp.concatenate([four, four], axis=0)
         tall = jnp.concatenate([eight] * (group // 8), axis=0)
-        qblk[r] = jnp.where(own_head, tall, 0.0).astype(BF16)
-        if r == 0:
-            for c in places:
-                c.wait()
+        block = jnp.where(own_head, tall, 0.0).astype(BF16)
         keys[r].wait()
-        raw = dot_t(qblk[r], k_v[r]) * HD ** (-0.5)
+        raw = dot_t(block, k_v[r]) * HD ** (-0.5)
         length = len_ref[r]
         seen = (position < length) & (
             (position < sink_ref[r]) | (length + s_row - position < win_ref[r]))
@@ -246,10 +258,29 @@
         top = jnp.max(scores, axis=1, keepdims=True)
         expo = jnp.where(seen, jnp.exp(scores - top), 0.0)
         total = jnp.sum(expo, axis=1, keepdims=True)
-        prob[r] = expo.astype(BF16)
-        m_full[NEW * r:NEW * (r + 1), :] = fold(jnp.broadcast_to(top, (group, width)))
-        l_full[NEW * r:NEW * (r + 1), :] = fold(jnp.broadcast_to(total, (group, width)))
-        if paired and r == 0:
+        values[r].wait()
+        out = jnp.dot(expo.astype(BF16), v_v[r], preferred_element_type=F32)
+        return (fold(out), fold(jnp.broadcast_to(top, (group, width))),
+                fold(jnp.broadcast_to(total, (group, width))))
+
+    def attend(g):
+        at = slice(8 * g, 8 * g + 8)
+        wait_results(q_all, qa_ss, qa_rs, g)
+        for h in range(heads):
+            q_full[at, head(h)] = q_all[h, at, 0:HD]
+        pieces = [weigh(each * g + i) for i in range(each)]
+        out, top, total = (jnp.concatenate(p, axis=0) for p in zip(*pieces))
+        for h in range(heads):
+            o_send[h, at, 0:HD] = out[:, head(h)]
+            o_send[h, at, HD:HD + SIDE] = top[:, h * HD:h * HD + SIDE]
+            o_send[h, at, HD + SIDE:PAD] = total[:, h * HD:h * HD + SIDE]
+        to_owners(o_send, o_part, o_ss, o_rs, start, g)
+
+    for c in places:
+        c.wait()
+    for g in range(halves):
+        attend(g)
+        if paired and g == 0:
             pair_parts().wait_recv()
             for i in range(half):
                 kv_sum[i] = kv_mid[i] + kv_send[side * half + i]
@@ -282,50 +313,42 @@
 
     on_owner(sum_new)
 
-    for r in range(count):
-        values[r].wait()
-        out = jnp.dot(prob[r], v_v[r], preferred_element_type=F32)
-        o_full[NEW * r:NEW * (r + 1), :] = fold(out)
-    for h in range(heads):
-        o_send[h, :, 0:HD] = o_full[:, head(h)]
-        o_send[h, :, HD:HD + SIDE] = m_full[:, h * HD:h * HD + SIDE]
-        o_send[h, :, HD + SIDE:PAD] = l_full[:, h * HD:h * HD + SIDE]
-    to_owners(o_send, o_part, o_ss, o_rs, start)
-    if paired:
-        for d in range(1, half):
-            arrived(lax.rem(me + 2 * d, seq))
-            forward(d).start()
-
-    def merge():
-        query = q_all[my_h][:, 0:HD].astype(BF16)
-        key = kv_all[my_h, 0][:, 0:HD].astype(BF16)
-        value = kv_all[my_h, 1][:, 0:HD].astype(BF16)
-        token = lax.broadcasted_iota(jnp.int32, (rows, rows), 0)
-        other = lax.broadcasted_iota(jnp.int32, (rows, rows), 1)
+    def merge(g):
+        at = slice(8 * g, 8 * g + 8)
+        query = q_all[my_h, at, 0:HD].astype(BF16)
+        key = kv_all[my_h, 0, at, 0:HD].astype(BF16)
+        value = kv_all[my_h, 1, at, 0:HD].astype(BF16)
+        token = lax.broadcasted_iota(jnp.int32, (8, 8), 0)
+        other = lax.broadcasted_iota(jnp.int32, (8, 8), 1)
         seen = (lax.div(token, jnp.int32(NEW)) == lax.div(other, jnp.int32(NEW))) & (other <= token)
         fresh = jnp.where(seen, dot_t(query, key) * HD ** (-0.5), NEG)
         own_top = jnp.max(fresh, axis=1, keepdims=True)
         expo = jnp.where(seen, jnp.exp(fresh - own_top), 0.0)
         own_sum = jnp.sum(expo, axis=1, keepdims=True)
         own_out = jnp.dot(expo.astype(BF16), value, preferred_element_type=F32)
-        o_part[me] = o_send[my_h]
-        wait_parts(o_send, o_part, o_rs, o_ss)
+        o_part[me, at] = o_send[my_h, at]
+        wait_parts(o_send, o_part, o_rs, o_ss, g)
         top = own_top
         for s in range(seq):
-            top = jnp.maximum(top, o_part[s][:, HD:HD + 1])
+            top = jnp.maximum(top, o_part[s, at, HD:HD + 1])
         factor = jnp.exp(own_top - top)
         total = own_sum * factor
         out = own_out * factor
         for s in range(seq):
-            piece = o_part[s]
+            piece = o_part[s, at]
             factor = jnp.exp(piece[:, HD:HD + 1] - top)
             out = out + piece[:, 0:HD] * factor
             total = total + piece[:, HD + SIDE:HD + SIDE + 1] * factor
-        a_all[my_h, :, 0:HD] = out / total
-        a_all[my_h, :, HD:PAD] = jnp.zeros((rows, PAD - HD), F32)
-        from_owner(a_all, a_ss, a_rs, start)
-
-    on_owner(merge)
+        a_all[my_h, at, 0:HD] = out / total
+        a_all[my_h, at, HD:PAD] = jnp.zeros((8, PAD - HD), F32)
+        from_owner(a_all, a_ss, a_rs, start, g)
+
+    for g in range(halves):
+        on_owner(functools.partial(merge, g))
+    if paired:
+        for d in range(1, half):
+            arrived(lax.rem(me + 2 * d, seq))
+            forward(d).start()
 
     if paired:
         for d in range(half):
@@ -336,7 +359,8 @@
         for j in range(2):
             kv_ref[j, :, head(h)] = kv_all[h, j, :, 0:HD]
     wo_load.wait()
-    wait_results(a_all, a_ss, a_rs)
+    for g in range(halves):
+        wait_results(a_all, a_ss, a_rs, g)
     for h in range(heads):
         a_full[:, head(h)] = a_all[h, :, 0:HD]
     t_part[mine_t] = dot_t(a_full[...].astype(BF16), wo_v[...])
@@ -349,9 +373,12 @@
 
     for d in range(1, tensor):
         to_tensor(d).start()
-    to_owners(q_send, q_part, q_ss, q_rs, wait_send)
-    to_owners(o_send, o_part, o_ss, o_rs, wait_send)
-    on_owner(lambda: from_owner(q_all, qa_ss, qa_rs, wait_send))
+    for g in range(halves):
+        to_owners(q_send, q_part, q_ss, q_rs, wait_send, g)
+    for g in range(halves):
+        to_owners(o_send, o_part, o_ss, o_rs, wait_send, g)
+    for g in range(halves):
+        on_owner(functools.partial(from_owner, q_all, qa_ss, qa_rs, wait_send, g))
     if paired:
         pair_parts().wait_send()
         for d in range(1, half):
@@ -362,7 +389,8 @@
     else:
         to_owners(kv_send, kv_part, kv_ss, kv_rs, wait_send)
         on_owner(lambda: from_owner(kv_all, kva_ss, kva_rs, wait_send))
-    on_owner(lambda: from_owner(a_all, a_ss, a_rs, wait_send))
+    for g in range(halves):
+        on_owner(functools.partial(from_owner, a_all, a_ss, a_rs, wait_send, g))
     for d in range(1, tensor):
         s = lax.rem(mine_t + d, tensor)
         pltpu.make_async_remote_copy(
@@ -385,7 +413,6 @@
     count, span, width = cached_key_rows.shape
     heads = width // HD
     out_width = output_weight.shape[1]
-    group = NEW * heads
     weights = jnp.transpose(query_key_value_weight, (1, 0, 2))
     wo = jnp.transpose(output_weight)
     hbm = pl.BlockSpec(memory_space=pltpu.HBM)
@@ -396,6 +423,7 @@
 
     dma = lambda n: pltpu.SemaphoreType.DMA((n,))
     ring = max(seq, heads)
+    twice = ring * (rows // 8)
     return pl.pallas_call(
         functools.partial(block_kernel, seq, tensor, heads, count),
         out_shape=(
@@ -411,23 +439,18 @@
             pltpu.VMEM((seq, rows, PAD), F32),
             pltpu.VMEM((heads, rows, PAD), F32),
             pltpu.VMEM((rows, width), F32),
-            pltpu.VMEM((count, group, width), BF16),
             pltpu.VMEM((heads, 2, rows, PAD), F32),
             pltpu.VMEM((heads // 2, 2, rows, PAD), F32),
             pltpu.VMEM((heads // 2, 2, rows, PAD), F32),
             pltpu.VMEM((seq, 2, rows, PAD), F32),
             pltpu.VMEM((heads, 2, rows, PAD), F32),
-            pltpu.VMEM((rows, width), F32),
-            pltpu.VMEM((rows, width), F32),
-            pltpu.VMEM((rows, width), F32),
             pltpu.VMEM((heads, rows, PAD), F32),
             pltpu.VMEM((seq, rows, PAD), F32),
             pltpu.VMEM((heads, rows, PAD), F32),
             pltpu.VMEM((rows, width), F32),
             pltpu.VMEM((tensor, rows, out_width), F32),
-            pltpu.VMEM((count, group, span), BF16),
             dma(11 + 2 * count),
-        ] + [dma(ring)] * 4 + [dma(1)] * 2 + [dma(ring)] * 8 + [dma(tensor)] * 2,
+        ] + [dma(twice)] * 4 + [dma(1)] * 2 + [dma(ring)] * 4 + [dma(twice)] * 4 + [dma(tensor)] * 2,
         compiler_params=pltpu.CompilerParams(
             collective_id=0, has_side_effects=True, vmem_limit_bytes=60 * 1024 * 1024,
         ),

time: 42.7 us -> 41.9 us (0.981)
  Pallas kernels: 38.9 us -> 38 us
    pallas_call x1, Pallas kernels: 38.9 us -> 38 us  [shards(): pl.pallas_call(functools.partial(block_kernel, seq, tensor, heads, count)...]
where the time goes in v3:
time: 41.9 us; the launch traced here: 41.7 us
  Pallas kernels  38 us (91%)
  local copies, waits for them, and re-layouts  3.02 us (7%)
  between operations  0.64 us (2%)
    pallas_call x1, Pallas kernels, shards(): pl.pallas_call(functools.partial(block_kernel, seq, tensor, heads, count)...  38 us
    unnamed x2, local copies, waits for them, and re-layouts  3.02 us

profile of v3, /device:TPU:0, one launch (start us, length us, event | category | flops | bytes accessed | tf_op | source)
XLA Modules:
  0.0 41.7 jit_solution(11193685842709474994)
XLA Ops:
  0.6 38.0 %shard_map.122 = (f32[16,448]{1,0:T(8,128)}, f32[2,16,1792]{2,1,0:T(8,128)}) custom-call(bf16[16,896]{1,0:T(8,128)(2,1)} %x_hbm.1, f32[896]{0:T(1024)} %g_hbm.1, bf16[3,896,1792]{2,1,0:T(8,128)(2,1)} %bitcast.2, bf16[896,128]{1,0:T(8,128)(2,1)} %down_hbm.1, bf16[128,1792]{1,0:T(8,128)(2,1)} %up_hbm.1, bf16[448,1792]{1,0:T(8,128)(2,1)} %bitcast.3, ...), custom_call_target="tpu_custom_call" | custom-call | tf_op jit(solution)/shard_map/pallas_call | solution.py:427
  38.6 1.4 %copy.15 = f32[16,448]{1,0:T(8,128)} copy(f32[16,448]{1,0:T(8,128)} %get-tuple-element.4) | data formatting | bytes 57344
  40.0 1.6 %copy.16 = f32[2,16,1792]{2,1,0:T(8,128)} copy(f32[2,16,1792]{2,1,0:T(8,128)} %get-tuple-element.5) | data formatting | bytes 458752

commit v4 on v3

--- a/solution.py
+++ b/solution.py
@@ -404,6 +404,15 @@
         to_tensor(d).wait_send()
 
 
+def place_kernel(mixed_hbm, kv_hbm, mixed_out, kv_out, sem):
+    copies = [pltpu.make_async_copy(kv_hbm.at[j], kv_out.at[j], sem.at[j]) for j in range(2)]
+    copies.append(pltpu.make_async_copy(mixed_hbm, mixed_out, sem.at[2]))
+    for c in copies:
+        c.start()
+    for c in copies:
+        c.wait()
+
+
 def shards(
     seq, tensor,
     features, input_norm_scale, query_key_value_weight, adapter_down_weight, adapter_up_weight,
@@ -424,7 +433,7 @@
     dma = lambda n: pltpu.SemaphoreType.DMA((n,))
     ring = max(seq, heads)
     twice = ring * (rows // 8)
-    return pl.pallas_call(
+    mixed, new_kv = pl.pallas_call(
         functools.partial(block_kernel, seq, tensor, heads, count),
         out_shape=(
             jax.ShapeDtypeStruct((rows, out_width), F32),
@@ -458,6 +467,15 @@
         features, input_norm_scale, weights, adapter_down_weight, adapter_up_weight, wo,
         cached_key_rows, cached_value_rows, lengths, sinks, windows,
     )
+    return pl.pallas_call(
+        place_kernel,
+        out_shape=(
+            jax.ShapeDtypeStruct(mixed.shape, F32), jax.ShapeDtypeStruct(new_kv.shape, F32)),
+        in_specs=[hbm] * 2,
+        out_specs=(hbm, hbm),
+        scratch_shapes=[dma(3)],
+        compiler_params=pltpu.CompilerParams(vmem_limit_bytes=60 * 1024 * 1024),
+    )(mixed, new_kv)
 
 
 def solution(mesh):

time: 41.9 us -> 47.9 us (1.14)
  Pallas kernels: 38 us -> 47.1 us
  local copies, waits for them, and re-layouts: 3.02 us -> 0 us
    pallas_call x0 -> x1, Pallas kernels: none -> 9.07 us  [shards(): pl.pallas_call(place_kernel, out_shape=(jax.ShapeDtypeStruct(mixed.shape,...]
    unnamed x2 -> x0, local copies, waits for them, and re-layouts: 3.02 us -> none
where the time goes in v4:
time: 47.9 us; the launch traced here: 47.7 us
  Pallas kernels  47.1 us (98%)
  between operations  0.64 us (1%)
    pallas_call x1, Pallas kernels, shards(): pl.pallas_call(functools.partial(block_kernel, seq, tensor, heads, count)...  38 us
    pallas_call x1, Pallas kernels, shards(): pl.pallas_call(place_kernel, out_shape=(jax.ShapeDtypeStruct(mixed.shape,...  9.07 us

profile of v4, /device:TPU:0, one launch (start us, length us, event | category | flops | bytes accessed | tf_op | source)
XLA Modules:
  0.0 47.7 jit_solution(4471530104618687036)
XLA Ops:
  0.6 38.0 %shard_map.122 = (f32[16,448]{1,0:T(8,128)}, f32[2,16,1792]{2,1,0:T(8,128)}) custom-call(bf16[16,896]{1,0:T(8,128)(2,1)} %x_hbm.1, f32[896]{0:T(1024)} %g_hbm.1, bf16[3,896,1792]{2,1,0:T(8,128)(2,1)} %bitcast.2, bf16[896,128]{1,0:T(8,128)(2,1)} %down_hbm.1, bf16[128,1792]{1,0:T(8,128)(2,1)} %up_hbm.1, bf16[448,1792]{1,0:T(8,128)(2,1)} %bitcast.3, ...), custom_call_target="tpu_custom_call" | custom-call | tf_op jit(solution)/shard_map/pallas_call | solution.py:436
  38.6 9.1 %shard_map.123 = (f32[16,448]{1,0:T(8,128)}, f32[2,16,1792]{2,1,0:T(8,128)}) custom-call(f32[16,448]{1,0:T(8,128)} %get-tuple-element.4.mixed_hbm, f32[2,16,1792]{2,1,0:T(8,128)} %get-tuple-element.5.kv_hbm), custom_call_target="tpu_custom_call" | custom-call | tf_op jit(solution)/shard_map/pallas_call | solution.py:470
